TPU v7x, 256 devices: a whole 4x4x8 slice. The times are simulated.
256 devices in a mesh: leaf: 64 (over z, x, core), node: 4 (over y).
Axes of the slice: x: 4, y: 4, z: 8, core: 2. Of those that a mesh axis runs over, the one named last changes fastest.
Arguments:
- leaf_blocks: float32 [131072, 512], P(('leaf', 'node')), as said below
- generators: float32 [3, 131072, 256], P(None, ('leaf', 'node'))
- right_side: float32 [131072, 256], P(('leaf', 'node'))
- tree_order: int32 [256, 512], P(('leaf', 'node')), may hold values from 0 to 511, each once within a row
Outputs:
- solution: float32 [131072, 256], P(('leaf', 'node'))
Inputs may be any that keep to these rules, and one draw needn't show every extreme that they name: `leaf_blocks`: each block of 512 rows, read as a square matrix, is symmetric positive definite.
All inputs are finite; a program needn't handle non-finite values.
Results may differ from a plain program's by a relative error of at most 0.0001.
Values sent between devices are 32-bit elements; how exact they have to be, the bound alone decides.
A program may use at most 64 MiB of HBM per device.

v0:
```python
import jax
import jax.numpy as jnp
from jax import lax
from jax.sharding import PartitionSpec as P

PRECISE = lax.Precision.HIGHEST


def from_partner(block, axis, apart):
    count = lax.axis_size(axis)
    route = []
    for low in range(count):
        high = low | 1 << apart
        if high != low and high < count:
            route += [(low, high), (high, low)]
    return lax.ppermute(block, axis, route)


def lower_solve(factor, values, transposed):
    return lax.linalg.triangular_solve(
        factor, values, left_side=True, lower=True, transpose_a=transposed
    )


def per_device(leaf_blocks, generators, right_side, tree_order):
    levels = generators.shape[0]
    rank = generators.shape[2]
    width = levels * rank
    ordered = jnp.take(right_side, tree_order[0], axis=0)
    leaf_factor = jnp.linalg.cholesky(leaf_blocks)
    stacked = jnp.concatenate([generators[height] for height in range(levels)] + [ordered], axis=1)
    solved = lower_solve(leaf_factor, stacked, False)
    partial_gram = jnp.einsum("ra,rb->ab", solved[:, :width], solved, precision=PRECISE)
    leaf_bits = lax.axis_size("leaf").bit_length() - 1
    current = lax.psum(partial_gram, "node")
    for bit_index in range(leaf_bits - levels):
        current = current + from_partner(current, "leaf", bit_index)
    identity = jnp.eye(rank, dtype=jnp.float32)
    factors = [None] * levels
    top_rows = [None] * levels
    for height in range(levels - 1, -1, -1):
        current = current + from_partner(current, "leaf", leaf_bits - height - 1)
        offset = height * rank
        header = current[offset : offset + rank, :]
        factor = jnp.linalg.cholesky(identity + header[:, offset : offset + rank])
        scaled = lower_solve(factor, header, False)
        factors[height] = factor
        top_rows[height] = header
        update = jnp.einsum("ra,rb->ab", scaled[:, :offset], scaled, precision=PRECISE)
        kept = current[:offset, :] - update
        current = jnp.concatenate([kept[:, :offset], kept[:, offset + rank :]], axis=1)
    coeffs = []
    for height in range(levels):
        offset = height * rank
        header = top_rows[height]
        target = header[:, offset + rank :]
        for upper in range(height):
            target = target - jnp.dot(
                header[:, upper * rank : (upper + 1) * rank], coeffs[upper], precision=PRECISE
            )
        middle = lower_solve(factors[height], target, False)
        coeffs.append(lower_solve(factors[height], middle, True))
    corrected = ordered
    for height in range(levels):
        corrected = corrected - jnp.dot(generators[height], coeffs[height], precision=PRECISE)
    tree_solution = lower_solve(leaf_factor, lower_solve(leaf_factor, corrected, False), True)
    return jnp.zeros_like(tree_solution).at[tree_order[0]].set(tree_solution)


def solution(mesh):
    return jax.shard_map(
        per_device,
        mesh=mesh,
        in_specs=(
            P(("leaf", "node"), None),
            P(None, ("leaf", "node"), None),
            P(("leaf", "node"), None),
            P(("leaf", "node"), None),
        ),
        out_specs=P(("leaf", "node"), None),
        check_vma=False,
    )
```

profile of v0, /device:TPU:1, one launch (start us, length us, event | category | flops | bytes accessed | tf_op | source)
XLA Modules:
  0.0 885.9 jit_solution(3918824648963202190)
XLA Ops:
  9.5 11.7 %cholesky.136 = f32[128,128]{1,0:T(8,128)S(1)} custom-call(f32[128,128]{1,0:T(8,128)S(1)} %cholesky.469), custom_call_target="Cholesky" | custom-call | tf_op jit(solution)/shard_map/jit(cholesky)/cholesky | solution.py:30
  33.7 11.7 %cholesky.159 = f32[128,128]{1,0:T(8,128)S(1)} custom-call(f32[128,128]{1,0:T(8,128)S(1)} %cholesky.473), custom_call_target="Cholesky" | custom-call | tf_op jit(solution)/shard_map/jit(cholesky)/cholesky | solution.py:30
  57.1 11.7 %cholesky.294 = f32[128,128]{1,0:T(8,128)S(1)} custom-call(f32[128,128]{1,0:T(8,128)S(1)} %cholesky.478), custom_call_target="Cholesky" | custom-call | tf_op jit(solution)/shard_map/jit(cholesky)/cholesky | solution.py:30
  80.7 11.7 %cholesky.307 = f32[128,128]{1,0:T(8,128)S(1)} custom-call(f32[128,128]{1,0:T(8,128)S(1)} %convolution_subtract_fusion.16), custom_call_target="Cholesky" | custom-call | tf_op jit(solution)/shard_map/jit(cholesky)/cholesky | solution.py:30
  96.3 12.1 %select_select_fusion = f32[512,512]{1,0:T(8,128)} fusion(f32[512,512]{1,0:T(8,128)S(1)} %get-tuple-element.137, pred[]{:T(512)S(6)} %cholesky.312), kind=kLoop, calls=%fused_computation.43 | loop fusion | flops 1048576 | bytes 2097153 | tf_op jit(solution)/shard_map/triangular_solve | solution.py:20
  108.4 13.7 %while.15 = (s32[]{:T(128)}, f32[512,512]{1,0:T(8,128)}, s32[4,2]{0,1:T(2,128)S(1)}, f32[4,128,128]{2,1,0:T(8,128)}, s32[]{:T(128)}) while((s32[]{:T(128)}, f32[512,512]{1,0:T(8,128)}, s32[4,2]{0,1:T(2,128)S(1)}, f32[4,128,128]{2,1,0:T(8,128)}, s32[]{:T(128)}) %tuple.102), condition=%wide.while_cond.2, body=%wide.while_body.2.sunk | while | flops 2 | bytes 132705 | solution.py:20
  122.1 40.1 %custom-call.50 = f32[4,128,128]{1,2,0:T(8,128)S(1)} custom-call(f32[4,128,128]{2,1,0:T(8,128)} %get-tuple-element.32), custom_call_target="InvertDiagBlocksLowerTriangular" | custom-call | tf_op jit(solution)/shard_map/triangular_solve | solution.py:20
  186.5 84.9 %all-reduce.4.cloned.1.call-done = f32[768,1024]{0,1:T(8,128)} async-done(((f32[768,1024]{0,1:T(8,128)}), f32[768,1024]{0,1:T(8,128)}) %all-reduce.4.cloned.1.call-update) | async-done | bytes 3145744 | tf_op jit(solution)/shard_map/psum | solution.py:35
  281.1 68.1 %collective-permute-done.1 = f32[768,1024]{0,1:T(8,128)S(1)} collective-permute-done((f32[768,1024]{0,1:T(8,128)S(1)}, f32[768,1024]{0,1:T(8,128)S(1)}, u32[]{:S(2)}, u32[]{:S(2)}) %collective-permute-start.1) | collective-permute-done | bytes 3145760 | tf_op jit(solution)/shard_map/ppermute | solution.py:16
  352.4 67.2 %collective-permute-done.2 = f32[768,1024]{0,1:T(8,128)S(1)} collective-permute-done((f32[768,1024]{0,1:T(8,128)S(1)}, f32[768,1024]{0,1:T(8,128)S(1)}, u32[]{:S(2)}, u32[]{:S(2)}) %collective-permute-start.2) | collective-permute-done | bytes 3145760 | tf_op jit(solution)/shard_map/ppermute | solution.py:16
  423.0 66.5 %collective-permute-done.3 = f32[768,1024]{0,1:T(8,128)} collective-permute-done((f32[768,1024]{0,1:T(8,128)}, f32[768,1024]{0,1:T(8,128)}, u32[]{:S(2)}, u32[]{:S(2)}) %collective-permute-start.3) | collective-permute-done | bytes 3145760 | tf_op jit(solution)/shard_map/ppermute | solution.py:16
  496.9 11.7 %cholesky.392 = f32[128,128]{1,0:T(8,128)S(1)} custom-call(f32[128,128]{1,0:T(8,128)S(1)} %cholesky.482), custom_call_target="Cholesky" | custom-call | tf_op jit(solution)/shard_map/jit(cholesky)/cholesky | solution.py:45
  522.0 11.7 %cholesky.402 = f32[128,128]{1,0:T(8,128)S(1)} custom-call(f32[128,128]{1,0:T(8,128)S(1)} %convolution_subtract_fusion.15), custom_call_target="Cholesky" | custom-call | tf_op jit(solution)/shard_map/jit(cholesky)/cholesky | solution.py:45
  545.1 20.5 %custom-call.51 = f32[2,128,128]{1,2,0:T(8,128)S(1)} custom-call(f32[2,128,128]{2,1,0:T(8,128)} %copy-done.18), custom_call_target="InvertDiagBlocksLowerTriangular" | custom-call | tf_op jit(solution)/shard_map/triangular_solve | solution.py:20
  575.8 67.9 %collective-permute-done.4 = f32[512,768]{0,1:T(8,128)} collective-permute-done((f32[512,768]{0,1:T(8,128)}, f32[512,768]{0,1:T(8,128)}, u32[]{:S(2)}, u32[]{:S(2)}) %collective-permute-start.4) | collective-permute-done | bytes 1572896 | tf_op jit(solution)/shard_map/ppermute | solution.py:16
  652.9 13.2 %cholesky.419 = f32[128,128]{1,0:T(8,128)} custom-call(f32[128,128]{1,0:T(8,128)} %cholesky.485), custom_call_target="Cholesky" | custom-call | tf_op jit(solution)/shard_map/jit(cholesky)/cholesky | solution.py:45
  669.1 11.3 %custom-call.65 = f32[1,128,128]{1,2,0:T(8,128)} custom-call(f32[1,128,128]{2,1,0:T(8,128)} %get-tuple-element.131), custom_call_target="InvertDiagBlocksLowerTriangular" | custom-call | tf_op jit(solution)/shard_map/jit(cholesky)/cholesky/custom-call.8 | solution.py:45
  683.8 13.2 %cholesky.429 = f32[128,128]{1,0:T(8,128)} custom-call(f32[128,128]{1,0:T(8,128)} %convolution_subtract_fusion.14), custom_call_target="Cholesky" | custom-call | tf_op jit(solution)/shard_map/jit(cholesky)/cholesky | solution.py:45
  710.3 21.1 %custom-call.52 = f32[2,128,128]{1,2,0:T(8,128)} custom-call(f32[2,128,128]{2,1,0:T(8,128)} %get-tuple-element.48), custom_call_target="InvertDiagBlocksLowerTriangular" | custom-call | tf_op jit(solution)/shard_map/triangular_solve | solution.py:20
  745.3 22.9 %collective-permute-done.5 = f32[256,512]{0,1:T(8,128)S(1)} collective-permute-done((f32[256,512]{0,1:T(8,128)S(1)}, f32[256,512]{0,1:T(8,128)S(1)}, u32[]{:S(2)}, u32[]{:S(2)}) %collective-permute-start.5) | collective-permute-done | bytes 524320 | tf_op jit(solution)/shard_map/ppermute | solution.py:16
  774.0 13.2 %cholesky.446 = f32[128,128]{1,0:T(8,128)} custom-call(f32[128,128]{1,0:T(8,128)} %cholesky.488), custom_call_target="Cholesky" | custom-call | tf_op jit(solution)/shard_map/jit(cholesky)/cholesky | solution.py:45
  790.3 11.3 %custom-call.66 = f32[1,128,128]{1,2,0:T(8,128)} custom-call(f32[1,128,128]{2,1,0:T(8,128)} %get-tuple-element.127), custom_call_target="InvertDiagBlocksLowerTriangular" | custom-call | tf_op jit(solution)/shard_map/jit(cholesky)/cholesky/custom-call.8 | solution.py:45
  805.0 13.2 %cholesky.456 = f32[128,128]{1,0:T(8,128)} custom-call(f32[128,128]{1,0:T(8,128)} %convolution_subtract_fusion.13), custom_call_target="Cholesky" | custom-call | tf_op jit(solution)/shard_map/jit(cholesky)/cholesky | solution.py:45
  831.4 21.3 %custom-call.68 = f32[2,128,128]{1,2,0:T(8,128)} custom-call(f32[2,128,128]{2,1,0:T(8,128)} %get-tuple-element.74), custom_call_target="InvertDiagBlocksLowerTriangular" | custom-call | tf_op jit(solution)/shard_map/triangular_solve/custom-call.13 | solution.py:20
  (226 shorter events, 246.1 us)
Async XLA Ops:
  6.5 158.3 %copy-start = (f32[512,256]{1,0:T(8,128)S(1)}, f32[512,256]{1,0:T(8,128)}, u32[]{:S(2)}) copy-start(f32[512,256]{1,0:T(8,128)} %param.13) | copy-start | bytes 1572868
  6.5 1.7 copy-start.9
  6.5 264.9 %all-reduce.4.cloned.1.call-start = ((), (), s32[]{:S(2)}) async-start(), calls=%async_computation | async-start | bytes 6291456 | tf_op jit(solution)/shard_map/psum | solution.py:35
  8.5 1.0 copy-start.11
  57.0 105.2 %copy-start.3 = (f32[3,512,256]{2,1,0:T(8,128)S(1)}, f32[3,512,256]{2,1,0:T(8,128)}, u32[]{:S(2)}) copy-start(f32[3,512,256]{2,1,0:T(8,128)} %param.12) | copy-start | bytes 4718596
  163.1 1.7 copy-start.19
  166.7 0.8 copy-start.7
  271.4 6.2 collective-permute-start
  279.8 69.4 %collective-permute-start.1 = (f32[768,1024]{0,1:T(8,128)S(1)}, f32[768,1024]{0,1:T(8,128)S(1)}, u32[]{:S(2)}, u32[]{:S(2)}) collective-permute-start(f32[768,1024]{0,1:T(8,128)S(1)} %add.117), channel_id=1, source_target_pairs={{0,8},{8,0},{4,12},{12,4},{16,24},{24,16},{20,28},{28,20},{32,40},... | collective-permute-start | bytes 9437192 | tf_op jit(solution)/shard_map/ppermute | solution.py:16
  349.6 70.0 %collective-permute-start.2 = (f32[768,1024]{0,1:T(8,128)S(1)}, f32[768,1024]{0,1:T(8,128)S(1)}, u32[]{:S(2)}, u32[]{:S(2)}) collective-permute-start(f32[768,1024]{0,1:T(8,128)S(1)} %add.118), channel_id=1, source_target_pairs={{0,16},{16,0},{4,20},{20,4},{8,24},{24,8},{12,28},{28,12},{32,48},... | collective-permute-start | bytes 9437192 | tf_op jit(solution)/shard_map/ppermute | solution.py:16
  421.7 67.8 %collective-permute-start.3 = (f32[768,1024]{0,1:T(8,128)}, f32[768,1024]{0,1:T(8,128)}, u32[]{:S(2)}, u32[]{:S(2)}) collective-permute-start(f32[768,1024]{0,1:T(8,128)} %add.119), channel_id=1, source_target_pairs={{0,32},{32,0},{4,36},{36,4},{8,40},{40,8},{12,44},{44,12},{16,48},... | collective-permute-start | bytes 9437192 | tf_op jit(solution)/shard_map/ppermute | solution.py:16
  570.8 1.0 copy-start.2
  571.8 1.3 copy-start.6
  573.1 70.6 %collective-permute-start.4 = (f32[512,768]{0,1:T(8,128)}, f32[512,768]{0,1:T(8,128)}, u32[]{:S(2)}, u32[]{:S(2)}) collective-permute-start(f32[512,768]{0,1:T(8,128)} %pad_maximum_fusion.1), channel_id=1, source_target_pairs={{0,64},{64,0},{4,68},{68,4},{8,72},{72,8},{12,76},{76,12},{16,80},... | collective-permute-start | bytes 4718600 | tf_op jit(solution)/shard_map/ppermute | solution.py:16
  738.8 29.4 %collective-permute-start.5 = (f32[256,512]{0,1:T(8,128)S(1)}, f32[256,512]{0,1:T(8,128)S(1)}, u32[]{:S(2)}, u32[]{:S(2)}) collective-permute-start(f32[256,512]{0,1:T(8,128)S(1)} %pad_maximum_fusion.2), channel_id=1, source_target_pairs={{0,128},{128,0},{4,132},{132,4},{8,136},{136,8},{12,140},{140,12},... | collective-permute-start | bytes 1572872 | tf_op jit(solution)/shard_map/ppermute | solution.py:16
  768.3 0.8 copy-start.10
  772.7 0.7 copy-start.17
  852.7 9.6 %copy-start.14 = (f32[2,128,128]{1,2,0:T(8,128)S(1)}, f32[2,128,128]{1,2,0:T(8,128)}, u32[]{:S(2)}) copy-start(f32[2,128,128]{1,2,0:T(8,128)} %custom-call.52) | copy-start | bytes 393220
  852.7 9.9 %copy-start.13 = (f32[256,256]{1,0:T(8,128)S(1)}, f32[256,256]{1,0:T(8,128)}, u32[]{:S(2)}) copy-start(f32[256,256]{1,0:T(8,128)} %get-tuple-element.344) | copy-start | bytes 786436
  858.8 5.4 copy-start.4
  863.0 3.2 copy-start.12
  865.2 3.6 copy-start.8
  867.7 2.5 copy-start.5
  872.7 5.9 copy-start.1
  (3 other events, 2.1 us)
Sparse Core Ops, SparseCore 0:
  186.6 84.7 all-reduce.3
where the time goes:
time: 897 us; the launch traced here: 886 us
  waiting for transfers between devices  383 us (43%)
  other arithmetic  340 us (38%)
  matrix products  68.7 us (8%)
  local copies, waits for them, and re-layouts  57.3 us (6%)
  between operations  21 us (2%)
  starting transfers between devices  15.2 us (2%)
    ppermute x6, waiting for transfers between devices, from_partner(): return lax.ppermute(block, axis, route)  298 us
    another operation x10, other arithmetic, lower_solve(): lax.linalg.triangular_solve(factor, values, left_side=True, lower=True, t...  120 us
    another operation x21, other arithmetic, per_device(): factor = jnp.linalg.cholesky(identity + header[:, offset:offset + rank])  119 us
    psum x1, waiting for transfers between devices, per_device(): current = lax.psum(partial_gram, 'node')  84.9 us
    another operation x14, other arithmetic, per_device(): leaf_factor = jnp.linalg.cholesky(leaf_blocks)  78.7 us
    another operation x45, matrix products, lower_solve(): lax.linalg.triangular_solve(factor, values, left_side=True, lower=True, t...  35.2 us
    another operation x24, local copies, waits for them, and re-layouts  26 us
  transfers between devices with their start and end apart: 7, of which 7 were waited for; matrix products, arithmetic and copies ran while one was open for 0% of the time, Pallas kernels for 0%

commit v1 on v0

v1 whole, which is shorter than its diff:
```python
import functools

import jax
import jax.numpy as jnp
from jax import lax
from jax.experimental import pallas as pl
from jax.experimental.pallas import tpu as pltpu
from jax.sharding import PartitionSpec as P

F32 = jnp.float32
BF16 = jnp.bfloat16
MESH = pl.DeviceIdType.MESH
NN = (((1,), (0,)), ((), ()))
NT = (((1,), (1,)), ((), ()))
TN = (((0,), (0,)), ((), ()))
BASE = 128
VMEM_LIMIT = 50 * 2**20


def split(value):
    high = value.astype(BF16)
    return high, (value - high.astype(F32)).astype(BF16)


def dot3(left, right, dims=NN):
    left_high, left_low = split(left)
    right_high, right_low = split(right)
    one = functools.partial(lax.dot_general, dimension_numbers=dims, preferred_element_type=F32)
    return one(left_high, right_high) + (one(left_high, right_low) + one(left_low, right_high))


def dot6(left, right, dims=NN):
    return lax.dot_general(
        left, right, dims, precision=lax.Precision.HIGHEST, preferred_element_type=F32
    )


def permute(one_hot, value, dims):
    high = value.astype(BF16)
    rest = value - high.astype(F32)
    middle = rest.astype(BF16)
    low = (rest - middle.astype(F32)).astype(BF16)
    one = functools.partial(lax.dot_general, dimension_numbers=dims, preferred_element_type=F32)
    return one(one_hot, high) + (one(one_hot, middle) + one(one_hot, low))


def ldl_factor(p):
    p = [list(row) for row in p]
    n = len(p)
    lower = [[None] * n for _ in range(n)]
    pivots = []
    for k in range(n):
        r = 1.0 / p[k][k]
        pivots.append(r)
        raw = [p[i][k] for i in range(n)] if k == 0 else [p[i][k] if i > k else None for i in range(n)]
        for i in range(k + 1, n):
            for j in range(k + 1, i + 1):
                p[i][j] = p[i][j] - r * (raw[i] * raw[j])
        for i in range(k + 1, n):
            lower[i][k] = raw[i] * r
    return lower, pivots


def ldl_solve(lower, pivots, rows):
    n = len(rows)
    y = list(rows)
    for k in range(n):
        for i in range(k + 1, n):
            y[i] = y[i] - lower[i][k] * y[k]
    z = [y[i] * pivots[i] for i in range(n)]
    for k in range(n - 1, -1, -1):
        for i in range(k):
            z[i] = z[i] - lower[k][i] * z[k]
    return z


def base_inverse(a, columns_ref, rows_ref):
    n = a.shape[0]
    count = n // 8
    lane = lax.broadcasted_iota(jnp.int32, (8, n), 1)
    sub = lax.broadcasted_iota(jnp.int32, (8, n), 0)
    a = [a[8 * v : 8 * v + 8, :] for v in range(count)]
    for kb in range(count):
        k = 8 * kb
        slot = kb % 2
        for j in range(8):
            columns_ref[slot, j] = jnp.broadcast_to(a[kb][:, k + j : k + j + 1], (8, n))
        inside = (lane >= k) & (lane < k + 8)
        rows_ref[slot] = jnp.where(inside, jnp.where(lane == sub + k, 1.0, 0.0), a[kb])
        p = [
            [jnp.broadcast_to(columns_ref[slot, j, i : i + 1, :], (8, n)) for j in range(i + 1)]
            for i in range(8)
        ]
        rows = [jnp.broadcast_to(rows_ref[slot, i : i + 1, :], (8, n)) for i in range(8)]
        q = ldl_solve(*ldl_factor(p), rows)
        own = q[0]
        for j in range(1, 8):
            own = jnp.where(sub == j, q[j], own)
        new = {kb: own}
        for m in range(1, count):
            v = (kb + m) % count
            terms = [jnp.broadcast_to(a[v][:, k + j : k + j + 1], (8, n)) * q[j] for j in range(8)]
            while len(terms) > 1:
                terms = [terms[i] + terms[i + 1] for i in range(0, len(terms), 2)]
            new[v] = jnp.where(inside, 0.0, a[v]) - terms[0]
        a = [new[v] for v in range(count)]
    return jnp.concatenate(a, axis=0)


def invert(a_ref, scratch):
    columns_ref, rows_ref, row_block, column_block = scratch
    n = a_ref.shape[0]
    eye = (
        lax.broadcasted_iota(jnp.int32, (BASE, BASE), 0)
        == lax.broadcasted_iota(jnp.int32, (BASE, BASE), 1)
    ).astype(F32)

    def step(kb, carry):
        own = pl.ds(pl.multiple_of(kb * BASE, BASE), BASE)
        pivot = base_inverse(a_ref[own, own], columns_ref, rows_ref)
        row_block[:, :n] = a_ref[own, :]
        row_block[:, own] = eye
        column_block[:n, :] = a_ref[:, own]
        a_ref[:, own] = jnp.zeros((n, BASE), F32)
        q = dot6(pivot, row_block[:, :n])
        a_ref[...] = a_ref[...] - dot6(column_block[:n, :], q)
        a_ref[own, :] = q
        return carry

    lax.fori_loop(0, n // BASE, step, 0)


def invert_scratch(n):
    return [
        pltpu.VMEM((2, 8, 8, BASE), F32),
        pltpu.VMEM((2, 8, BASE), F32),
        pltpu.VMEM((BASE, n), F32),
        pltpu.VMEM((n, BASE), F32),
    ]


PAIRS = ((2, 2), (1, 2), (0, 2), (2, 3), (1, 1), (0, 1), (1, 3), (0, 0), (0, 3))


def one_hot_of(order_ref):
    n = order_ref.shape[1]
    target = lax.broadcasted_iota(jnp.int32, (n, n), 0)
    return jnp.where(target == order_ref[...], 1.0, 0.0).astype(BF16)


def leaf_kernel(leaf_ref, gens_ref, rhs_ref, order_ref, x_ref, gram_ref, inverse, *scratch):
    inverse[...] = leaf_ref[...]
    invert(inverse, scratch)
    high, low = split(inverse[...])
    one = functools.partial(lax.dot_general, dimension_numbers=NN, preferred_element_type=F32)

    def apply(value):
        value_high, value_low = split(value)
        return one(high, value_high) + (one(high, value_low) + one(low, value_high))

    for level in range(3):
        x_ref[level] = apply(gens_ref[level])
    x_ref[3] = apply(permute(one_hot_of(order_ref), rhs_ref[...], TN))
    for index, (a, b) in enumerate(PAIRS):
        product = dot3(gens_ref[a], x_ref[b], TN)
        for half in range(2):
            gram_ref[index, half] = product[:, half * 128 : half * 128 + 128]


def leaf(leaf_blocks, generators, right_side, order):
    rows, rank = leaf_blocks.shape[0], generators.shape[2]
    return pl.pallas_call(
        leaf_kernel,
        out_shape=(
            jax.ShapeDtypeStruct((4, rows, rank), F32),
            jax.ShapeDtypeStruct((9, 2, rank, 128), F32),
        ),
        scratch_shapes=[pltpu.VMEM((rows, rows), F32)] + invert_scratch(rows),
        compiler_params=pltpu.CompilerParams(vmem_limit_bytes=VMEM_LIMIT),
        name="leaf",
    )(leaf_blocks, generators, right_side, order)


def place():
    leaf_index = lax.axis_index("leaf")
    return leaf_index // 8, (leaf_index // 2) % 4, leaf_index % 2, lax.axis_index("node")


def device(z, x, core, y):
    return ((z * 4 + x) * 2 + core, y)


def owned_rows(half, x, core, y):
    return core * 128 + ((x * 4 + y) if half == 0 else (y * 4 + x)) * 8


def exchange_kernel(reduce, blocks, header, z_bit, *refs):
    if reduce:
        (in_ref, head_ref, rest_ref, total, from_core, from_one, from_two, from_z, one, two) = refs[:10]
        core_sem, one_sem, two_sem, z_sem, first_sem, second_sem, last_sem = refs[10:]
    else:
        in_ref, head_ref, rest_ref, total, from_z = refs[:5]
        z_sem, first_sem, second_sem, last_sem = refs[5:]
    z, x, core, y = place()
    across = device(z, x, 1 - core, y)
    z_partner = device(z ^ (1 << z_bit), x, core, y)

    def along(axis, step):
        if axis == "x":
            return lax.rem(x + step, 4), device(z, lax.rem(x + step, 4), core, y)
        return lax.rem(y + step, 4), device(z, x, core, lax.rem(y + step, 4))

    barrier = pltpu.get_barrier_semaphore()
    partners = [across, z_partner] + [along(axis, step)[1] for axis in "xy" for step in (1, 2, 3)]
    for partner in partners:
        pl.semaphore_signal(barrier, inc=1, device_id=partner, device_id_type=MESH)
    pl.semaphore_wait(barrier, len(partners))

    def send(source, target, sems, to):
        copy = pltpu.make_async_remote_copy(
            src_ref=source, dst_ref=target, send_sem=sems.at[0], recv_sem=sems.at[1],
            device_id=to, device_id_type=MESH,
        )
        copy.start()
        return copy

    first_axis, second_axis = ("x", "y"), ("y", "x")
    mine = {"x": x, "y": y}
    if reduce:
        copy = send(in_ref.at[:, :, pl.ds((1 - core) * 128, 128), :], from_core, core_sem, across)
        copy.wait()
        one[...] = in_ref[:, :, pl.ds(core * 128, 128), :] + from_core[...]
        copies = []
        for step in (1, 2, 3):
            for half in range(2):
                index, to = along(first_axis[half], step)
                copies.append(
                    send(one.at[:, half, pl.ds(index * 32, 32), :], from_one.at[step - 1, half],
                         one_sem.at[step - 1, half], to)
                )
        for copy in copies:
            copy.wait()
        for half in range(2):
            own = one[:, half, pl.ds(mine[first_axis[half]] * 32, 32), :]
            two[:, half] = (own + from_one[0, half]) + (from_one[1, half] + from_one[2, half])
        copies = []
        for step in (1, 2, 3):
            for half in range(2):
                index, to = along(second_axis[half], step)
                copies.append(
                    send(two.at[:, half, pl.ds(index * 8, 8), :], from_two.at[step - 1, half],
                         two_sem.at[step - 1, half], to)
                )
        for copy in copies:
            copy.wait()
        for half in range(2):
            own = two[:, half, pl.ds(mine[second_axis[half]] * 8, 8), :]
            total[:, half] = (own + from_two[0, half]) + (from_two[1, half] + from_two[2, half])
        source = total
    else:
        source = in_ref
    copy = send(source, from_z, z_sem, z_partner)
    copy.wait()
    sums = source[...] + from_z[...]
    if blocks > header:
        rest_ref[...] = sums[header:]
    for half in range(2):
        head_ref[:, half, pl.ds(owned_rows(half, x, core, y), 8), :] = sums[:header, half]
    copies = []
    for step in (1, 2, 3):
        for half in range(2):
            part = head_ref.at[:, half, pl.ds(owned_rows(half, x, core, y), 8), :]
            copies.append(
                send(part, part, first_sem.at[step - 1, half], along(second_axis[half], step)[1])
            )
    for copy in copies:
        copy.wait()
    copies = []
    for step in (1, 2, 3):
        for half in range(2):
            part = head_ref.at[:, half, pl.ds(core * 128 + mine[first_axis[half]] * 32, 32), :]
            copies.append(
                send(part, part, second_sem.at[step - 1, half], along(first_axis[half], step)[1])
            )
    for copy in copies:
        copy.wait()
    part = head_ref.at[:, :, pl.ds(core * 128, 128), :]
    send(part, part, last_sem, across).wait()


def exchange(value, header, z_bit, reduce, collective_id):
    blocks = value.shape[0]
    dma = pltpu.SemaphoreType.DMA
    scratch = []
    if reduce:
        scratch = [
            pltpu.VMEM((blocks, 2, 8, 128), F32),
            pltpu.VMEM((blocks, 2, 128, 128), F32),
            pltpu.VMEM((3, 2, blocks, 32, 128), F32),
            pltpu.VMEM((3, 2, blocks, 8, 128), F32),
            pltpu.VMEM((blocks, 2, 8, 128), F32),
            pltpu.VMEM((blocks, 2, 128, 128), F32),
            pltpu.VMEM((blocks, 2, 32, 128), F32),
            dma((2,)), dma((3, 2, 2)), dma((3, 2, 2)),
        ]
    else:
        scratch = [pltpu.VMEM((8, 128), F32), pltpu.VMEM((blocks, 2, 8, 128), F32)]
    scratch += [dma((2,)), dma((3, 2, 2)), dma((3, 2, 2)), dma((2,))]
    rest = max(blocks - header, 1)
    return pl.pallas_call(
        functools.partial(exchange_kernel, reduce, blocks, header, z_bit),
        out_shape=(
            jax.ShapeDtypeStruct((header, 2, 256, 128), F32),
            jax.ShapeDtypeStruct((rest, 2, 8, 128), F32),
        ),
        in_specs=[pl.BlockSpec(memory_space=pltpu.VMEM)],
        out_specs=(pl.BlockSpec(memory_space=pltpu.VMEM), pl.BlockSpec(memory_space=pltpu.VMEM)),
        scratch_shapes=scratch,
        compiler_params=pltpu.CompilerParams(
            collective_id=collective_id, has_side_effects=True, vmem_limit_bytes=VMEM_LIMIT
        ),
        name="exchange",
    )(value)


def whole(ref, index):
    return jnp.concatenate([ref[index, 0], ref[index, 1]], axis=1)


def plus_identity(value):
    n = value.shape[0]
    eye = lax.broadcasted_iota(jnp.int32, (n, n), 0) == lax.broadcasted_iota(jnp.int32, (n, n), 1)
    return value + jnp.where(eye, 1.0, 0.0)


def level_kernel(level, head_ref, rest_ref, out_ref, scaled_ref, inverse, *scratch):
    z, x, core, y = place()
    inverse[...] = plus_identity(whole(head_ref, 0))
    invert(inverse, scratch)
    for upper in range(level):
        scaled_ref[upper] = dot3(inverse[...], whole(head_ref, level - upper), NT)
    scaled_ref[level] = dot3(inverse[...], whole(head_ref, level + 1))
    index = 0
    for a in range(level - 1, -1, -1):
        for b in list(range(a, -1, -1)) + [level]:
            for half in range(2):
                own = pl.ds(owned_rows(half, x, core, y), 8)
                if b == level or b == a:
                    left, right = a, b
                else:
                    left, right = b, a
                rows = jnp.concatenate(
                    [head_ref[level - left, 0, own, :], head_ref[level - left, 1, own, :]], axis=1
                )
                update = dot3(rows, scaled_ref[right, :, half * 128 : half * 128 + 128])
                out_ref[index, half] = rest_ref[index, half] - update
            index += 1


def tree_level(level, head, rest):
    return pl.pallas_call(
        functools.partial(level_kernel, level),
        out_shape=(
            jax.ShapeDtypeStruct(rest.shape, F32),
            jax.ShapeDtypeStruct((level + 1, 256, 256), F32),
        ),
        scratch_shapes=[pltpu.VMEM((256, 256), F32)] + invert_scratch(256),
        compiler_params=pltpu.CompilerParams(vmem_limit_bytes=VMEM_LIMIT),
        name="level",
    )(head, rest)


def finish_kernel(head_ref, one_ref, two_ref, x_ref, order_ref, out_ref, inverse, *scratch):
    inverse[...] = plus_identity(whole(head_ref, 0))
    invert(inverse, scratch)
    c0 = dot3(inverse[...], whole(head_ref, 1))
    c1 = one_ref[1] - dot3(one_ref[0], c0)
    c2 = two_ref[2] - dot3(two_ref[0], c0) - dot3(two_ref[1], c1)
    x = x_ref[3] - dot3(x_ref[0], c0) - dot3(x_ref[1], c1) - dot3(x_ref[2], c2)
    out_ref[...] = permute(one_hot_of(order_ref), x, NN)


def finish(head, one, two, x, order):
    return pl.pallas_call(
        finish_kernel,
        out_shape=jax.ShapeDtypeStruct(x.shape[1:], F32),
        scratch_shapes=[pltpu.VMEM((256, 256), F32)] + invert_scratch(256),
        compiler_params=pltpu.CompilerParams(vmem_limit_bytes=VMEM_LIMIT),
        name="finish",
    )(head, one, two, x, order)


def per_device(leaf_blocks, generators, right_side, tree_order):
    x, gram = leaf(leaf_blocks, generators, right_side, tree_order)
    head, rest = exchange(gram, 4, 0, True, 0)
    rest, two = tree_level(2, head, rest)
    head, rest = exchange(rest, 3, 1, False, 1)
    rest, one = tree_level(1, head, rest)
    head, _ = exchange(rest, 2, 2, False, 2)
    return finish(head, one, two, x, tree_order)


def solution(mesh):
    return jax.shard_map(
        per_device,
        mesh=mesh,
        in_specs=(
            P(("leaf", "node"), None),
            P(None, ("leaf", "node"), None),
            P(("leaf", "node"), None),
            P(("leaf", "node"), None),
        ),
        out_specs=P(("leaf", "node"), None),
        check_vma=False,
    )
```

time: 897 us -> 143 us (0.16); the launches traced: 886 us -> 143 us
  waiting for transfers between devices: 383 us -> 0 us
  other arithmetic: 340 us -> 0 us
  Pallas kernels: 0 us -> 136 us
  matrix products: 68.7 us -> 0 us
  local copies, waits for them, and re-layouts: 57.3 us -> 6.03 us
  between operations: 21 us -> 0.06 us
  starting transfers between devices: 15.2 us -> 0 us
    another operation x45 -> x0, other arithmetic: 318 us -> none  [the longest x10 120 us: lower_solve(): lax.linalg.triangular_solve(factor, values, left_side=True, lower=True, t...]
    ppermute x6 -> x0, waiting for transfers between devices: 298 us -> none  [from_partner(): return lax.ppermute(block, axis, route)]
    pallas_call x0 -> x7, Pallas kernels: none -> 136 us  [the longest x3 72.3 us: exchange(): pl.pallas_call(functools.partial(exchange_kernel, reduce, blocks, header,...]
    psum x1 -> x0, waiting for transfers between devices: 84.9 us -> none  [per_device(): current = lax.psum(partial_gram, 'node')]
    another operation x57 -> x0, matrix products: 50.3 us -> none  [the longest x45 35.2 us: lower_solve(): lax.linalg.triangular_solve(factor, values, left_side=True, lower=True, t...]
    another operation x42 -> x0, local copies, waits for them, and re-layouts: 38.2 us -> none
    dot_general x9 -> x0, matrix products: 18.3 us -> none  [the longest x1 7.86 us: per_device(): jnp.einsum('ra,rb->ab', solved[:, :width], solved, precision=PRECISE)]
    ppermute x6 -> x0, starting transfers between devices: 15.2 us -> none  [from_partner(): return lax.ppermute(block, axis, route)]
  transfers between devices with their start and end apart: 7 -> 0, of which waited for: 7 -> 0; matrix products, arithmetic and copies ran while one was open for 0% -> 0% of each run, Pallas kernels for 0% -> 0%
where the time goes in v1:
time: 143 us
  Pallas kernels  136 us (95%)
  local copies, waits for them, and re-layouts  6.03 us (4%)
    pallas_call x3, Pallas kernels, exchange(): pl.pallas_call(functools.partial(exchange_kernel, reduce, blocks, header,...  72.3 us
    pallas_call x1, Pallas kernels, leaf(): pl.pallas_call(leaf_kernel, out_shape=(jax.ShapeDtypeStruct((4, rows, ran...  29.9 us
    pallas_call x2, Pallas kernels, tree_level(): pl.pallas_call(functools.partial(level_kernel, level), out_shape=(jax.Sha...  21 us
    pallas_call x1, Pallas kernels, finish(): pl.pallas_call(finish_kernel, out_shape=jax.ShapeDtypeStruct(x.shape[1:],...  13.3 us
    unnamed x14, local copies, waits for them, and re-layouts  6.03 us

profile of v1, /device:TPU:1, one launch (start us, length us, event | category | flops | bytes accessed | tf_op | source)
XLA Modules:
  0.0 142.6 jit_solution(7451752136520669744)
XLA Ops:
  0.0 0.0 copy-start.2
  0.0 1.4 copy-done.2
  1.4 0.0 copy-start.3
  1.4 1.2 copy-done.3
  2.6 0.0 copy-start.4
  2.6 1.0 copy-done.4
  3.7 0.0 copy-start.5
  3.7 0.7 copy-done.5
  4.4 29.9 %leaf.1 = (f32[4,512,256]{2,1,0:T(8,128)}, f32[9,2,256,128]{3,2,1,0:T(8,128)}) custom-call(f32[512,512]{1,0:T(8,128)S(1)} %copy-done.3, f32[3,512,256]{2,1,0:T(8,128)S(1)} %copy-done.2, f32[512,256]{1,0:T(8,128)S(1)} %copy-done.4, s32[1,512]{1,0:T(1,128)S(1)} %copy-done.5), custom_call_target="tpu_custom_call" | custom-call | tf_op jit(solution)/shard_map/leaf/pallas_call | solution.py:172
  34.2 0.0 copy-start
  34.2 1.7 %copy-done = f32[9,2,256,128]{3,2,1,0:T(8,128)S(1)} copy-done((f32[9,2,256,128]{3,2,1,0:T(8,128)S(1)}, f32[9,2,256,128]{3,2,1,0:T(8,128)}, u32[]{:S(2)}) %copy-start) | copy-done | bytes 2359320
  35.9 0.0 copy-start.1
  35.9 0.0 copy-start.6
  35.9 36.3 %exchange.3 = (f32[4,2,256,128]{3,2,1,0:T(8,128)S(1)}, f32[5,2,8,128]{3,2,1,0:T(8,128)S(1)}) custom-call(f32[9,2,256,128]{3,2,1,0:T(8,128)S(1)} %copy-done), custom_call_target="tpu_custom_call" | custom-call | tf_op jit(solution)/shard_map/exchange/pallas_call | solution.py:310
  72.2 10.7 %level.2 = (f32[5,2,8,128]{3,2,1,0:T(8,128)S(1)}, f32[3,256,256]{2,1,0:T(8,128)S(1)}) custom-call(f32[4,2,256,128]{3,2,1,0:T(8,128)S(1)} %get-tuple-element.17.head_ref, f32[5,2,8,128]{3,2,1,0:T(8,128)S(1)} %get-tuple-element.18.rest_ref), custom_call_target="tpu_custom_call" | custom-call | tf_op jit(solution)/shard_map/level/pallas_call | solution.py:361
  82.9 17.7 %exchange.4 = (f32[3,2,256,128]{3,2,1,0:T(8,128)S(1)}, f32[2,2,8,128]{3,2,1,0:T(8,128)S(1)}) custom-call(f32[5,2,8,128]{3,2,1,0:T(8,128)S(1)} %get-tuple-element.19.refs_0_), custom_call_target="tpu_custom_call" | custom-call | tf_op jit(solution)/shard_map/exchange/pallas_call | solution.py:310
  100.6 10.3 %level.3 = (f32[2,2,8,128]{3,2,1,0:T(8,128)S(1)}, f32[2,256,256]{2,1,0:T(8,128)S(1)}) custom-call(f32[3,2,256,128]{3,2,1,0:T(8,128)S(1)} %get-tuple-element.20.head_ref, f32[2,2,8,128]{3,2,1,0:T(8,128)S(1)} %get-tuple-element.21.rest_ref), custom_call_target="tpu_custom_call" | custom-call | tf_op jit(solution)/shard_map/level/pallas_call | solution.py:361
  110.9 18.3 %exchange.5 = (f32[2,2,256,128]{3,2,1,0:T(8,128)S(1)}, f32[1,2,8,128]{3,2,1,0:T(8,128)}) custom-call(f32[2,2,8,128]{3,2,1,0:T(8,128)S(1)} %get-tuple-element.22.refs_0_), custom_call_target="tpu_custom_call" | custom-call | tf_op jit(solution)/shard_map/exchange/pallas_call | solution.py:310
  129.2 0.0 copy-done.1
  129.2 0.0 copy-done.6
  129.2 13.3 %finish.1 = f32[512,256]{1,0:T(8,128)} custom-call(f32[2,2,256,128]{3,2,1,0:T(8,128)S(1)} %get-tuple-element.23.head_ref, f32[2,256,256]{2,1,0:T(8,128)S(1)} %get-tuple-element.24.one_ref, f32[3,256,256]{2,1,0:T(8,128)S(1)} %get-tuple-element.25.two_ref, f32[4,512,256]{2,1,0:T(8,128)S(1)} %copy-done.1, s32[1,512]{1,0:T(1,128)S(1)} %copy-done.6), custom_call_target="tpu_custom_call" | custom-call | tf_op jit(solution)/shard_map/finish/pallas_call | solution.py:384
Async XLA Ops:
  0.0 1.4 copy-start.2
  1.4 1.2 copy-start.3
  2.6 1.0 copy-start.4
  3.7 0.7 copy-start.5
  34.2 1.7 %copy-start = (f32[9,2,256,128]{3,2,1,0:T(8,128)S(1)}, f32[9,2,256,128]{3,2,1,0:T(8,128)}, u32[]{:S(2)}) copy-start(f32[9,2,256,128]{3,2,1,0:T(8,128)} %get-tuple-element.16.refs_0_) | copy-start | bytes 7077892
  35.9 93.3 %copy-start.1 = (f32[4,512,256]{2,1,0:T(8,128)S(1)}, f32[4,512,256]{2,1,0:T(8,128)}, u32[]{:S(2)}) copy-start(f32[4,512,256]{2,1,0:T(8,128)} %get-tuple-element.26.x_ref) | copy-start | bytes 6291460
  35.9 93.3 %copy-start.6 = (s32[1,512]{1,0:T(1,128)S(1)}, s32[1,512]{1,0:T(1,128)}, u32[]{:S(2)}) copy-start(s32[1,512]{1,0:T(1,128)} %order_ref.3) | copy-start | bytes 6148

commit v2 on v0

v2 whole, which is shorter than its diff:
```python
import functools

import jax
import jax.numpy as jnp
from jax import lax
from jax.experimental import pallas as pl
from jax.experimental.pallas import tpu as pltpu
from jax.sharding import PartitionSpec as P

F32 = jnp.float32
BF16 = jnp.bfloat16
MESH = pl.DeviceIdType.MESH
NN = (((1,), (0,)), ((), ()))
NT = (((1,), (1,)), ((), ()))
TN = (((0,), (0,)), ((), ()))
BASE = 128
VMEM_LIMIT = 50 * 2**20


def split(value):
    high = value.astype(BF16)
    return high, (value - high.astype(F32)).astype(BF16)


def dot3(left, right, dims=NN):
    left_high, left_low = split(left)
    right_high, right_low = split(right)
    one = functools.partial(lax.dot_general, dimension_numbers=dims, preferred_element_type=F32)
    return one(left_high, right_high) + (one(left_high, right_low) + one(left_low, right_high))


def dot6(left, right, dims=NN):
    return lax.dot_general(
        left, right, dims, precision=lax.Precision.HIGHEST, preferred_element_type=F32
    )


def permute(one_hot, value, dims):
    high = value.astype(BF16)
    rest = value - high.astype(F32)
    middle = rest.astype(BF16)
    low = (rest - middle.astype(F32)).astype(BF16)
    one = functools.partial(lax.dot_general, dimension_numbers=dims, preferred_element_type=F32)
    return one(one_hot, high) + (one(one_hot, middle) + one(one_hot, low))


def ldl_factor(p):
    p = [list(row) for row in p]
    n = len(p)
    lower = [[None] * n for _ in range(n)]
    pivots = []
    for k in range(n):
        r = 1.0 / p[k][k]
        pivots.append(r)
        raw = [p[i][k] for i in range(n)] if k == 0 else [p[i][k] if i > k else None for i in range(n)]
        for i in range(k + 1, n):
            for j in range(k + 1, i + 1):
                p[i][j] = p[i][j] - r * (raw[i] * raw[j])
        for i in range(k + 1, n):
            lower[i][k] = raw[i] * r
    return lower, pivots


def ldl_solve(lower, pivots, rows):
    n = len(rows)
    y = list(rows)
    for k in range(n):
        for i in range(k + 1, n):
            y[i] = y[i] - lower[i][k] * y[k]
    z = [y[i] * pivots[i] for i in range(n)]
    for k in range(n - 1, -1, -1):
        for i in range(k):
            z[i] = z[i] - lower[k][i] * z[k]
    return z


def base_inverse(a, columns_ref, rows_ref):
    n = a.shape[0]
    lane8 = lax.broadcasted_iota(jnp.int32, (8, n), 1)
    sub8 = lax.broadcasted_iota(jnp.int32, (8, n), 0)
    lane = lax.broadcasted_iota(jnp.int32, (n, n), 1)
    for kb in range(n // 8):
        k = 8 * kb
        slot = kb % 2
        own = a[k : k + 8, :]
        for j in range(8):
            columns_ref[slot, j] = jnp.broadcast_to(own[:, k + j : k + j + 1], (8, n))
        inside = (lane8 >= k) & (lane8 < k + 8)
        rows_ref[slot] = jnp.where(inside, jnp.where(lane8 == sub8 + k, 1.0, 0.0), own)
        p = [
            [jnp.broadcast_to(columns_ref[slot, j, i : i + 1, :], (8, n)) for j in range(i + 1)]
            for i in range(8)
        ]
        rows = [jnp.broadcast_to(rows_ref[slot, i : i + 1, :], (8, n)) for i in range(8)]
        q = ldl_solve(*ldl_factor(p), rows)
        own = q[0]
        for j in range(1, 8):
            own = jnp.where(sub8 == j, q[j], own)
        rest = jnp.where((lane >= k) & (lane < k + 8), 0.0, a)
        terms = [
            jnp.broadcast_to(a[:, k + j : k + j + 1], (n, n))
            * jnp.broadcast_to(q[j][0:1, :], (n, n))
            for j in range(8)
        ]
        while len(terms) > 1:
            terms = [terms[i] + terms[i + 1] for i in range(0, len(terms), 2)]
        rest = rest - terms[0]
        parts = [rest[:k]] if k else []
        parts.append(own)
        if k + 8 < n:
            parts.append(rest[k + 8 :])
        a = jnp.concatenate(parts, axis=0)
    return a


def invert(a_ref, scratch):
    columns_ref, rows_ref, row_block, column_block = scratch
    n = a_ref.shape[0]
    eye = (
        lax.broadcasted_iota(jnp.int32, (BASE, BASE), 0)
        == lax.broadcasted_iota(jnp.int32, (BASE, BASE), 1)
    ).astype(F32)

    def step(kb, carry):
        own = pl.ds(pl.multiple_of(kb * BASE, BASE), BASE)
        pivot = base_inverse(a_ref[own, own], columns_ref, rows_ref)
        row_block[:, :n] = a_ref[own, :]
        row_block[:, own] = eye
        column_block[:n, :] = a_ref[:, own]
        a_ref[:, own] = jnp.zeros((n, BASE), F32)
        q = dot6(pivot, row_block[:, :n])
        a_ref[...] = a_ref[...] - dot6(column_block[:n, :], q)
        a_ref[own, :] = q
        return carry

    lax.fori_loop(0, n // BASE, step, 0)


PAIRS = ((2, 2), (1, 2), (0, 2), (2, 3), (1, 1), (0, 1), (1, 3), (0, 0), (0, 3))


def place():
    leaf_index = lax.axis_index("leaf")
    return leaf_index // 8, (leaf_index // 2) % 4, leaf_index % 2, lax.axis_index("node")


def device(z, x, core, y):
    return ((z * 4 + x) * 2 + core, y)


class Links:
    def __init__(self, sems):
        self.sems = sems
        self.used = 0
        self.sent = []
        self.z, self.x, self.core, self.y = place()
        self.across = device(self.z, self.x, 1 - self.core, self.y)
        self.mine = {"x": self.x, "y": self.y}

    def along(self, axis, step):
        if axis == "x":
            index = lax.rem(self.x + step, 4)
            return index, device(self.z, index, self.core, self.y)
        index = lax.rem(self.y + step, 4)
        return index, device(self.z, self.x, self.core, index)

    def above(self, bit):
        return device(self.z ^ (1 << bit), self.x, self.core, self.y)

    def partners(self):
        near = [self.along(axis, step)[1] for axis in "xy" for step in (1, 2, 3)]
        return near + [self.across] + [self.above(bit) for bit in range(3)]

    def owned(self, half):
        index = self.x * 4 + self.y if half == 0 else self.y * 4 + self.x
        return pl.ds(self.core * 128 + index * 8, 8)

    def send(self, source, target, to):
        copy = pltpu.make_async_remote_copy(
            src_ref=source, dst_ref=target, send_sem=self.sems.at[self.used, 0],
            recv_sem=self.sems.at[self.used, 1], device_id=to, device_id_type=MESH,
        )
        self.used += 1
        copy.start()
        self.sent.append(copy)
        return copy


FIRST, SECOND = ("x", "y"), ("y", "x")


class Group:
    def __init__(self, links, blocks, bit, part, from_z, head=None, plane=None):
        self.links, self.blocks, self.bit = links, blocks, bit
        self.part, self.from_z, self.head, self.plane = part, from_z, head, plane
        self.pending = []

    def arrived(self):
        for copy in self.pending:
            copy.wait_recv()
        self.pending = []

    def over_cores(self):
        gram, from_core = self.plane[:2]
        links, blocks = self.links, self.blocks
        other = pl.ds((1 - links.core) * 128, 128)
        self.pending = [
            links.send(gram.at[blocks, :, other, :], from_core.at[blocks], links.across)
        ]

    def over_first(self):
        gram, from_core, one, from_one = self.plane[:4]
        links, blocks = self.links, self.blocks
        self.arrived()
        one[blocks] = gram[blocks, :, pl.ds(links.core * 128, 128), :] + from_core[blocks]
        for step in (1, 2, 3):
            for half in range(2):
                index, to = links.along(FIRST[half], step)
                source = one.at[blocks, half, pl.ds(index * 32, 32), :]
                self.pending.append(
                    links.send(source, from_one.at[step - 1, half, blocks], to)
                )

    def over_second(self):
        one, from_one, two, from_two = self.plane[2:]
        links, blocks = self.links, self.blocks
        self.arrived()
        for half in range(2):
            own = one[blocks, half, pl.ds(links.mine[FIRST[half]] * 32, 32), :]
            two[blocks, half] = (own + from_one[0, half, blocks]) + (
                from_one[1, half, blocks] + from_one[2, half, blocks]
            )
        for step in (1, 2, 3):
            for half in range(2):
                index, to = links.along(SECOND[half], step)
                source = two.at[blocks, half, pl.ds(index * 8, 8), :]
                self.pending.append(
                    links.send(source, from_two.at[step - 1, half, blocks], to)
                )

    def over_planes(self):
        links, blocks = self.links, self.blocks
        if self.plane is not None:
            two, from_two = self.plane[4:]
            self.arrived()
            for half in range(2):
                own = two[blocks, half, pl.ds(links.mine[SECOND[half]] * 8, 8), :]
                self.part[blocks, half] = (own + from_two[0, half, blocks]) + (
                    from_two[1, half, blocks] + from_two[2, half, blocks]
                )
        self.pending = [
            links.send(self.part.at[blocks], self.from_z.at[blocks], links.above(self.bit))
        ]

    def summed(self):
        self.arrived()
        return self.part[self.blocks] + self.from_z[self.blocks]

    def spread(self, half_rows, axes):
        for step in (1, 2, 3):
            for half in range(2):
                part = self.head.at[self.blocks, half, half_rows[half], :]
                self.pending.append(
                    self.links.send(part, part, self.links.along(axes[half], step)[1])
                )

    def gather_second(self):
        links = self.links
        sums = self.summed()
        for half in range(2):
            self.head[self.blocks, half, links.owned(half), :] = sums[:, half]
        self.spread([links.owned(half) for half in range(2)], SECOND)

    def gather_first(self):
        links = self.links
        self.arrived()
        self.spread(
            [pl.ds(links.core * 128 + links.mine[FIRST[half]] * 32, 32) for half in range(2)], FIRST
        )

    def gather_cores(self):
        links = self.links
        self.arrived()
        part = self.head.at[self.blocks, :, pl.ds(links.core * 128, 128), :]
        self.pending = [links.send(part, part, links.across)]


def one_hot_of(order_ref):
    n = order_ref.shape[1]
    target = lax.broadcasted_iota(jnp.int32, (n, n), 0)
    return jnp.where(target == order_ref[...], 1.0, 0.0).astype(BF16)


def whole(ref, index):
    return jnp.concatenate([ref[index, 0], ref[index, 1]], axis=1)


def plus_identity(value):
    n = value.shape[0]
    eye = lax.broadcasted_iota(jnp.int32, (n, n), 0) == lax.broadcasted_iota(jnp.int32, (n, n), 1)
    return value + jnp.where(eye, 1.0, 0.0)


def kernel(
    leaf_hbm, gens_hbm, rhs_hbm, order_hbm, out_hbm,
    inverse, gens, rhs, order, x, moved, result,
    gram, from_core, one, from_one, two, from_two,
    part2, from2, head2, part1, from1, head1, part0, from0, head0,
    small, scaled, columns_ref, rows_ref, row_block, column_block,
    in_sems, out_sem, sems,
):
    scratch = (columns_ref, rows_ref, row_block, column_block)
    links = Links(sems)
    loads = [
        pltpu.make_async_copy(source, target, in_sems.at[i])
        for i, (source, target) in enumerate(
            ((leaf_hbm, inverse), (gens_hbm, gens), (rhs_hbm, rhs), (order_hbm, order))
        )
    ]
    for load in loads:
        load.start()
    barrier = pltpu.get_barrier_semaphore()
    partners = links.partners()
    for partner in partners:
        pl.semaphore_signal(barrier, inc=1, device_id=partner, device_id_type=MESH)

    loads[0].wait()
    invert(inverse, scratch)
    for load in loads[1:]:
        load.wait()

    def apply(value):
        return dot3(inverse[...], value)

    def product(index):
        a, b = PAIRS[index]
        value = dot3(gens[a], x[b], TN)
        for half in range(2):
            gram[index, half] = value[:, half * 128 : half * 128 + 128]

    plane = (gram, from_core, one, from_one, two, from_two)
    g0, g1, g2 = (
        Group(links, blocks, 0, part2, from2, head2, plane)
        for blocks in (pl.ds(0, 1), pl.ds(1, 3), pl.ds(4, 5))
    )
    x[2] = apply(gens[2])
    product(0)
    pl.semaphore_wait(barrier, len(partners))
    g0.over_cores()
    product(1)
    product(2)
    g0.over_first()
    one_hot = one_hot_of(order)
    x[3] = apply(permute(one_hot, rhs[...], TN))
    product(3)
    g1.over_cores()
    g0.over_second()
    x[1] = apply(gens[1])
    product(4)
    product(5)
    g0.over_planes()
    g1.over_first()
    x[0] = apply(gens[0])
    product(6)
    g0.gather_second()
    product(7)
    product(8)
    g2.over_cores()
    g1.over_second()
    g0.gather_first()
    moved[2] = permute(one_hot, x[2], NN)
    g1.over_planes()
    g2.over_first()
    g0.gather_cores()
    moved[1] = permute(one_hot, x[1], NN)
    g1.gather_second()
    g2.over_second()
    moved[0] = permute(one_hot, x[0], NN)
    g1.gather_first()
    g2.over_planes()
    g1.gather_cores()
    g0.arrived()
    small[...] = plus_identity(whole(head2, 0))
    invert(small, scratch)
    g1.arrived()
    rest2 = g2.summed()

    def slices(target, index, head, a, b, scaled_b, old):
        for half in range(2):
            own = links.owned(half)
            rows = jnp.concatenate([head[a, 0, own, :], head[a, 1, own, :]], axis=1)
            update = dot3(rows, scaled_b[:, half * 128 : half * 128 + 128])
            target[index, half] = old[index, half] - update

    h0, h1, h2 = (
        Group(links, blocks, 1, part1, from1, head1)
        for blocks in (pl.ds(0, 1), pl.ds(1, 2), pl.ds(3, 2))
    )
    h2.head = None
    scaled[1] = dot3(small[...], whole(head2, 1), NT)
    slices(part1, 0, head2, 1, 1, scaled[1], rest2)
    h0.over_planes()
    scaled[2] = dot3(small[...], whole(head2, 3))
    slices(part1, 1, head2, 2, 1, scaled[1], rest2)
    slices(part1, 2, head2, 1, 3, scaled[2], rest2)
    h1.over_planes()
    scaled[0] = dot3(small[...], whole(head2, 2), NT)
    slices(part1, 3, head2, 2, 0, scaled[0], rest2)
    slices(part1, 4, head2, 2, 3, scaled[2], rest2)
    h2.over_planes()
    moved[1] = moved[1] - dot3(moved[2], scaled[1])
    h0.gather_second()
    h1.gather_second()
    moved[0] = moved[0] - dot3(moved[2], scaled[0])
    h0.gather_first()
    h1.gather_first()
    moved[3] = permute(one_hot_of(order), x[3], NN) - dot3(moved[2], scaled[2])
    h0.gather_cores()
    h1.gather_cores()
    h0.arrived()
    small[...] = plus_identity(whole(head1, 0))
    invert(small, scratch)
    h1.arrived()
    rest1 = h2.summed()

    k0, k1 = (
        Group(links, blocks, 2, part0, from0, head0) for blocks in (pl.ds(0, 1), pl.ds(1, 1))
    )
    scaled[0] = dot3(small[...], whole(head1, 1), NT)
    slices(part0, 0, head1, 1, 0, scaled[0], rest1)
    k0.over_planes()
    scaled[1] = dot3(small[...], whole(head1, 2))
    slices(part0, 1, head1, 1, 3, scaled[1], rest1)
    k1.over_planes()
    moved[0] = moved[0] - dot3(moved[1], scaled[0])
    k0.gather_second()
    k1.gather_second()
    moved[3] = moved[3] - dot3(moved[1], scaled[1])
    k0.gather_first()
    k1.gather_first()
    k0.gather_cores()
    k1.gather_cores()
    k0.arrived()
    small[...] = plus_identity(whole(head0, 0))
    invert(small, scratch)
    k1.arrived()
    coeff = dot3(small[...], whole(head0, 1))
    result[...] = moved[3] - dot3(moved[0], coeff)
    store = pltpu.make_async_copy(result, out_hbm, out_sem)
    store.start()
    for copy in links.sent:
        copy.wait_send()
    store.wait()


COPIES = 3 * (1 + 6 + 6 + 1) + 2 * 13 + 3 + 2 * 13 + 2 + 2 * 13


def per_device(leaf_blocks, generators, right_side, tree_order):
    rows, rank = leaf_blocks.shape[0], generators.shape[2]
    dma = pltpu.SemaphoreType.DMA

    def buffer(*shape):
        return pltpu.VMEM(shape, F32)

    scratch = [
        buffer(rows, rows), buffer(3, rows, rank), buffer(rows, rank), pltpu.VMEM((1, rows), jnp.int32),
        buffer(4, rows, rank), buffer(4, rows, rank), buffer(rows, rank),
        buffer(9, 2, 256, 128), buffer(9, 2, 128, 128), buffer(9, 2, 128, 128),
        buffer(3, 2, 9, 32, 128), buffer(9, 2, 32, 128), buffer(3, 2, 9, 8, 128),
        buffer(9, 2, 8, 128), buffer(9, 2, 8, 128), buffer(4, 2, 256, 128),
        buffer(5, 2, 8, 128), buffer(5, 2, 8, 128), buffer(3, 2, 256, 128),
        buffer(2, 2, 8, 128), buffer(2, 2, 8, 128), buffer(2, 2, 256, 128),
        buffer(rank, rank), buffer(3, rank, rank),
        buffer(2, 8, 8, BASE), buffer(2, 8, BASE), buffer(BASE, rows), buffer(rows, BASE),
        dma((4,)), dma(()), dma((COPIES, 2)),
    ]
    hbm = pl.BlockSpec(memory_space=pltpu.MemorySpace.HBM)
    return pl.pallas_call(
        kernel,
        out_shape=jax.ShapeDtypeStruct(right_side.shape, F32),
        in_specs=[hbm] * 4,
        out_specs=hbm,
        scratch_shapes=scratch,
        compiler_params=pltpu.CompilerParams(
            collective_id=0, has_side_effects=True, vmem_limit_bytes=VMEM_LIMIT
        ),
        name="solve",
    )(leaf_blocks, generators, right_side, tree_order)


def solution(mesh):
    return jax.shard_map(
        per_device,
        mesh=mesh,
        in_specs=(
            P(("leaf", "node"), None),
            P(None, ("leaf", "node"), None),
            P(("leaf", "node"), None),
            P(("leaf", "node"), None),
        ),
        out_specs=P(("leaf", "node"), None),
        check_vma=False,
    )
```

time: 897 us -> 119 us (0.13); the launches traced: 886 us -> 118 us
  waiting for transfers between devices: 383 us -> 0 us
  other arithmetic: 340 us -> 0 us
  Pallas kernels: 0 us -> 113 us
  matrix products: 68.7 us -> 0 us
  local copies, waits for them, and re-layouts: 57.3 us -> 5.15 us
  between operations: 21 us -> 0.01 us
  starting transfers between devices: 15.2 us -> 0 us
    another operation x45 -> x0, other arithmetic: 318 us -> none  [the longest x10 120 us: lower_solve(): lax.linalg.triangular_solve(factor, values, left_side=True, lower=True, t...]
    ppermute x6 -> x0, waiting for transfers between devices: 298 us -> none  [from_partner(): return lax.ppermute(block, axis, route)]
    pallas_call x0 -> x1, Pallas kernels: none -> 113 us  [per_device(): pl.pallas_call(kernel, out_shape=jax.ShapeDtypeStruct(right_side.shape, F...]
    psum x1 -> x0, waiting for transfers between devices: 84.9 us -> none  [per_device(): current = lax.psum(partial_gram, 'node')]
    another operation x57 -> x0, matrix products: 50.3 us -> none  [the longest x45 35.2 us: lower_solve(): lax.linalg.triangular_solve(factor, values, left_side=True, lower=True, t...]
    another operation x42 -> x0, local copies, waits for them, and re-layouts: 38.2 us -> none
    dot_general x9 -> x0, matrix products: 18.3 us -> none  [the longest x1 7.86 us: per_device(): jnp.einsum('ra,rb->ab', solved[:, :width], solved, precision=PRECISE)]
    ppermute x6 -> x0, starting transfers between devices: 15.2 us -> none  [from_partner(): return lax.ppermute(block, axis, route)]
  transfers between devices with their start and end apart: 7 -> 0, of which waited for: 7 -> 0; matrix products, arithmetic and copies ran while one was open for 0% -> 0% of each run, Pallas kernels for 0% -> 0%
where the time goes in v2:
time: 119 us; the launch traced here: 118 us
  Pallas kernels  113 us (95%)
  local copies, waits for them, and re-layouts  5.15 us (4%)
    pallas_call x1, Pallas kernels, per_device(): pl.pallas_call(kernel, out_shape=jax.ShapeDtypeStruct(right_side.shape, F...  113 us
    unnamed x9, local copies, waits for them, and re-layouts  5.15 us

profile of v2, /device:TPU:1, one launch (start us, length us, event | category | flops | bytes accessed | tf_op | source)
XLA Modules:
  0.0 118.4 jit_solution(17038858234305154371)
XLA Ops:
  0.0 0.0 copy-start
  0.0 1.4 %copy-done = f32[3,512,256]{2,1,0:T(8,128)S(1)} copy-done((f32[3,512,256]{2,1,0:T(8,128)S(1)}, f32[3,512,256]{2,1,0:T(8,128)}, u32[]{:S(2)}) %copy-start) | copy-done | bytes 1572888
  1.4 0.0 copy-start.1
  1.4 1.2 %copy-done.1 = f32[512,512]{1,0:T(8,128)S(1)} copy-done((f32[512,512]{1,0:T(8,128)S(1)}, f32[512,512]{1,0:T(8,128)}, u32[]{:S(2)}) %copy-start.1) | copy-done | bytes 1048600
  2.6 0.0 copy-start.2
  2.6 1.0 copy-done.2
  3.7 0.0 copy-start.3
  3.7 0.7 copy-done.3
  4.4 113.3 %solve.1 = f32[512,256]{1,0:T(8,128)S(1)} custom-call(f32[512,512]{1,0:T(8,128)S(1)} %copy-done.1, f32[3,512,256]{2,1,0:T(8,128)S(1)} %copy-done, f32[512,256]{1,0:T(8,128)S(1)} %copy-done.2, s32[1,512]{1,0:T(1,128)S(1)} %copy-done.3), custom_call_target="tpu_custom_call" | custom-call | tf_op jit(solution)/shard_map/solve/pallas_call | solution.py:479
  117.6 0.8 copy.6
Async XLA Ops:
  0.0 1.4 %copy-start = (f32[3,512,256]{2,1,0:T(8,128)S(1)}, f32[3,512,256]{2,1,0:T(8,128)}, u32[]{:S(2)}) copy-start(f32[3,512,256]{2,1,0:T(8,128)} %gens_hbm.1) | copy-start | bytes 4718596
  1.4 1.2 %copy-start.1 = (f32[512,512]{1,0:T(8,128)S(1)}, f32[512,512]{1,0:T(8,128)}, u32[]{:S(2)}) copy-start(f32[512,512]{1,0:T(8,128)} %leaf_hbm.1) | copy-start | bytes 3145732
  2.6 1.0 copy-start.2
  3.7 0.7 copy-start.3
